TPU v7x, 256 devices: a whole 4x4x8 slice. The times are simulated.
256 devices in a mesh: diag: 32 (over z, y_hi, core), off: 8 (over y_lo, x).
Axes of the slice: x: 4, y: 4 (y_hi: 2, y_lo: 2; y = y_hi * 2 + y_lo), z: 8, core: 2. Of those that a mesh axis runs over, the one named last changes fastest.
Arguments:
- vectors: bfloat16 [16, 524288], P(None, ('diag', 'off')), may hold values from -6 to 6
- tile_blocks: bfloat16 [81920, 128, 128], P(('diag', 'off')), may hold values from -0.078125 to 0.078125
- tile_index: int32 [81920, 2], P(('diag', 'off')), may hold values from 0 to 127
- tile_live: int32 [81920, 2], P(('diag', 'off')), may hold values from 32 to 128
- tile_count: int32 [256], P(('diag', 'off')), may hold values from 40 to 320, as said below
Outputs:
- image: float32 [16, 524288], P(None, ('diag', 'off'))
Inputs may be any that keep to these rules, and one draw needn't show every extreme that they name: `tile_count`: the live slots of a device are its first ones; some device has all 320 slots live and another only 40.
All inputs are finite; a program needn't handle non-finite values.
Results may differ from a plain program's by a relative error of at most 0.0003.
Values may be sent and summed in bfloat16 or wider, within the bound.
No kernel may reach another device: no remote copies, remote signals or barrier semaphores. Data moves between devices by JAX's collectives and lax.ppermute only.
A program may use at most 64 MiB of HBM per device.

v0:
```python
import jax
import jax.numpy as jnp
from jax import lax
from jax.sharding import PartitionSpec as P


def passed_along(block, axis, distance):
    devices = range(lax.axis_size(axis))
    route = [((i - distance) % len(devices), i) for i in devices]
    return lax.ppermute(block, axis, route)


def per_device(vectors, tile_blocks, tile_index, tile_live, tile_count):
    width_off = lax.axis_size("off")
    levels = width_off.bit_length() - 1
    column_index = lax.axis_index("off")
    row_segment = lax.all_gather(vectors, "off", axis=1, tiled=True)
    nvecs, seg_len = row_segment.shape
    tile_len = tile_blocks.shape[1]
    nblocks = seg_len // tile_len
    col_segment = row_segment
    for level in range(levels):
        arrived = passed_along(col_segment, "diag", -(1 << level))
        col_segment = jnp.where(column_index >> level & 1 == 1, arrived, col_segment)
    x_rows = row_segment.reshape(nvecs, nblocks, tile_len)
    x_cols = col_segment.reshape(nvecs, nblocks, tile_len)
    block_size = 32
    live_count = tile_count[0]
    rounds = (live_count + block_size - 1) // block_size
    within = jnp.arange(tile_len, dtype=jnp.int32)

    def one_round(round_index, carry):
        row_acc, col_acc = carry
        start = round_index * block_size
        blocks = lax.dynamic_slice_in_dim(tile_blocks, start, block_size, 0)
        index_part = lax.dynamic_slice_in_dim(tile_index, start, block_size, 0)
        live_part = lax.dynamic_slice_in_dim(tile_live, start, block_size, 0)
        alive = start + jnp.arange(block_size, dtype=jnp.int32) < live_count
        row_keep = (within[None, :] < live_part[:, 0:1]) & alive[:, None]
        col_keep = within[None, :] < live_part[:, 1:2]
        from_cols = jnp.take(x_cols, index_part[:, 1], axis=1) * col_keep.astype(jnp.bfloat16)[None]
        forward = jnp.einsum("ktj,tij->kti", from_cols, blocks, preferred_element_type=jnp.float32)
        forward = forward * row_keep.astype(jnp.float32)[None]
        from_rows = jnp.take(x_rows, index_part[:, 0], axis=1) * row_keep.astype(jnp.bfloat16)[None]
        backward = jnp.einsum("kti,tij->ktj", from_rows, blocks, preferred_element_type=jnp.float32)
        backward = backward * col_keep.astype(jnp.float32)[None]
        row_acc = row_acc.at[:, index_part[:, 0]].add(forward)
        col_acc = col_acc.at[:, index_part[:, 1]].add(backward)
        return (row_acc, col_acc)

    zeros_acc = jnp.zeros((nvecs, nblocks, tile_len), jnp.float32)
    row_part, col_part = lax.fori_loop(0, rounds, one_round, (zeros_acc, zeros_acc))
    row_part = row_part.reshape(nvecs, seg_len)
    col_part = col_part.reshape(nvecs, seg_len)
    carried = col_part
    for level in range(levels):
        arrived = passed_along(carried, "diag", 1 << level)
        carried = jnp.where(column_index >> level & 1 == 1, arrived, carried)
    result = lax.psum_scatter(row_part + carried, "off", scatter_dimension=1, tiled=True)
    return result


def solution(mesh):
    placed = (
        P(None, ("diag", "off")),
        P(("diag", "off"), None, None),
        P(("diag", "off"), None),
        P(("diag", "off"), None),
        P(("diag", "off")),
    )
    return jax.shard_map(
        per_device, mesh=mesh, in_specs=placed, out_specs=P(None, ("diag", "off")), check_vma=False
    )
```

profile of v0, /device:TPU:32, one launch (start us, length us, event | category | flops | bytes accessed | tf_op | source)
XLA Modules:
  0.0 300.0 jit_solution(15141334728513711590)
XLA Ops:
  6.5 29.6 %all_gather.3 = bf16[16,16384]{1,0:T(8,128)(2,1)S(1)} all-gather(bf16[16,2048]{1,0:T(8,128)(2,1)} %param.9), channel_id=1, replica_groups=mesh['diag'=32,'off'=8] {'off'}, dimensions={1}, use_global_device_ids=true | all-gather | bytes 589824 | tf_op jit(solution)/shard_map/all_gather | solution.py:17
  36.1 6.7 %collective-permute-done = bf16[16,16384]{1,0:T(8,128)(2,1)S(1)} collective-permute-done((bf16[16,16384]{1,0:T(8,128)(2,1)S(1)}, bf16[16,16384]{1,0:T(8,128)(2,1)S(1)}, u32[]{:S(2)}, u32[]{:S(2)}) %collective-permute-start) | collective-permute-done | bytes 524320 | tf_op jit(solution)/shard_map/ppermute | solution.py:10
  42.9 2.5 collective-permute-start.1
  45.4 11.6 %collective-permute-done.1 = bf16[16,16384]{1,0:T(8,128)(2,1)S(1)} collective-permute-done((bf16[16,16384]{1,0:T(8,128)(2,1)S(1)}, bf16[16,16384]{1,0:T(8,128)(2,1)S(1)}, u32[]{:S(2)}, u32[]{:S(2)}) %collective-permute-start.1) | collective-permute-done | bytes 524320 | tf_op jit(solution)/shard_map/ppermute | solution.py:10
  57.0 5.1 %collective-permute-start.2 = (bf16[16,16384]{1,0:T(8,128)(2,1)S(1)}, bf16[16,16384]{1,0:T(8,128)(2,1)S(1)}, u32[]{:S(2)}, u32[]{:S(2)}) collective-permute-start(bf16[16,16384]{1,0:T(8,128)(2,1)S(1)} %broadcast_select_fusion.3), channel_id=1, source_target_pairs={{32,0},{40,8},{48,16},{56,24},{64,32},{72,40},{80,48},{88,56},{96,... | collective-permute-start | bytes 1572872 | tf_op jit(solution)/shard_map/ppermute | solution.py:10
  62.9 9.4 %collective-permute-done.2 = bf16[16,16384]{1,0:T(8,128)(2,1)S(1)} collective-permute-done((bf16[16,16384]{1,0:T(8,128)(2,1)S(1)}, bf16[16,16384]{1,0:T(8,128)(2,1)S(1)}, u32[]{:S(2)}, u32[]{:S(2)}) %collective-permute-start.2) | collective-permute-done | bytes 524320 | tf_op jit(solution)/shard_map/ppermute | solution.py:10
  72.3 0.9 copy_bitcast_fusion.2
  73.4 65.5 %while.14 = (s32[]{:T(128)}, f32[16,128,128]{2,0,1:T(8,128)S(1)}, f32[16,128,128]{2,0,1:T(8,128)S(1)}, s32[]{:T(128)}, s32[320,2]{0,1:T(2,128)}, /*index=5*/bf16...) while((s32[]{:T(128)}, f32[16,128,128]{2,0,1:T(8,128)S(1)}, ...), condition=%wide.region_3.5_spmd.clone.clone, body=%wide.region_0.4_spmd.clone.clone.sunk | while | flops 34306692 | bytes 5091207 | solution.py:52
  74.1 0.8 constant_dynamic-slice_fusion.3
  75.6 1.7 fusion.42
  77.3 1.6 gather_fusion
  78.9 1.9 fusion.41
  80.9 1.7 scatter_fusion
  82.6 1.7 scatter_fusion.1
  85.0 0.8 constant_dynamic-slice_fusion.3
  86.6 1.7 fusion.42
  88.2 1.6 gather_fusion
  89.9 1.9 fusion.41
  91.8 1.7 scatter_fusion
  93.5 1.7 scatter_fusion.1
  95.9 0.8 constant_dynamic-slice_fusion.3
  97.5 1.7 fusion.42
  99.1 1.6 gather_fusion
  100.8 1.9 fusion.41
  102.7 1.7 scatter_fusion
  104.4 1.7 scatter_fusion.1
  106.8 0.8 constant_dynamic-slice_fusion.3
  108.4 1.7 fusion.42
  110.1 1.6 gather_fusion
  111.7 1.9 fusion.41
  113.6 1.7 scatter_fusion
  115.3 1.7 scatter_fusion.1
  119.3 1.7 fusion.42
  121.0 1.6 gather_fusion
  122.6 1.9 fusion.41
  124.5 1.7 scatter_fusion
  126.3 1.7 scatter_fusion.1
  130.2 1.7 fusion.42
  131.9 1.6 gather_fusion
  133.6 1.9 fusion.41
  135.5 1.7 scatter_fusion
  137.2 1.7 scatter_fusion.1
  139.1 16.6 %collective-permute-done.3 = f32[16,16384]{1,0:T(8,128)S(1)} collective-permute-done((f32[16,16384]{1,0:T(8,128)S(1)}, f32[16,16384]{1,0:T(8,128)S(1)}, u32[]{:S(2)}, u32[]{:S(2)}) %collective-permute-start.3) | collective-permute-done | bytes 1048608 | tf_op jit(solution)/shard_map/ppermute | solution.py:10
  155.8 47.0 %collective-permute-start.4 = (f32[16,16384]{1,0:T(8,128)S(1)}, f32[16,16384]{1,0:T(8,128)S(1)}, u32[]{:S(2)}, u32[]{:S(2)}) collective-permute-start(f32[16,16384]{1,0:T(8,128)S(1)} %broadcast_select_fusion), channel_id=1, source_target_pairs={{240,0},{248,8},{0,16},{8,24},{16,32},{24,40},{32,48},{40,56},{48,... | collective-permute-start | bytes 3145736 | tf_op jit(solution)/shard_map/ppermute | solution.py:10
  202.8 19.0 %collective-permute-done.4 = f32[16,16384]{1,0:T(8,128)S(1)} collective-permute-done((f32[16,16384]{1,0:T(8,128)S(1)}, f32[16,16384]{1,0:T(8,128)S(1)}, u32[]{:S(2)}, u32[]{:S(2)}) %collective-permute-start.4) | collective-permute-done | bytes 1048608 | tf_op jit(solution)/shard_map/ppermute | solution.py:10
  222.0 20.5 %collective-permute-done.5 = f32[16,16384]{1,0:T(8,128)S(1)} collective-permute-done((f32[16,16384]{1,0:T(8,128)S(1)}, f32[16,16384]{1,0:T(8,128)S(1)}, u32[]{:S(2)}, u32[]{:S(2)}) %collective-permute-start.5) | collective-permute-done | bytes 1048608 | tf_op jit(solution)/shard_map/ppermute | solution.py:10
  242.5 1.2 bitcast_add_fusion
  243.7 49.4 %reduce-scatter.2.cloned.1.call-done = f32[16,2048]{1,0:T(8,128)} async-done(((f32[16,16384]{1,0:T(8,128)}), f32[16,2048]{1,0:T(8,128)}) %reduce-scatter.2.cloned.1.call-update) | async-done | bytes 131088 | tf_op jit(solution)/shard_map/reduce_scatter | solution.py:59
  (69 shorter events, 10.9 us)
Async XLA Ops:
  6.5 286.6 %reduce-scatter.2.cloned.1.call-start = ((), (), s32[]{:S(2)}) async-start(), calls=%async_computation.1 | async-start | bytes 1179648 | tf_op jit(solution)/shard_map/reduce_scatter | solution.py:59
  36.1 6.7 %collective-permute-start = (bf16[16,16384]{1,0:T(8,128)(2,1)S(1)}, bf16[16,16384]{1,0:T(8,128)(2,1)S(1)}, u32[]{:S(2)}, u32[]{:S(2)}) collective-permute-start(bf16[16,16384]{1,0:T(8,128)(2,1)S(1)} %all_gather.3), channel_id=1, source_target_pairs={{8,0},{16,8},{24,16},{32,24},{40,32},{48,40},{56,48},{64,56},{72,6... | collective-permute-start | bytes 1572872 | tf_op jit(solution)/shard_map/ppermute | solution.py:10
  42.9 14.1 %collective-permute-start.1 = (bf16[16,16384]{1,0:T(8,128)(2,1)S(1)}, bf16[16,16384]{1,0:T(8,128)(2,1)S(1)}, u32[]{:S(2)}, u32[]{:S(2)}) collective-permute-start(bf16[16,16384]{1,0:T(8,128)(2,1)S(1)} %broadcast_select_fusion.1), channel_id=1, source_target_pairs={{16,0},{24,8},{32,16},{40,24},{48,32},{56,40},{64,48},{72,56},{80,... | collective-permute-start | bytes 1572872 | tf_op jit(solution)/shard_map/ppermute | solution.py:10
  57.0 15.3 %collective-permute-start.2 = (bf16[16,16384]{1,0:T(8,128)(2,1)S(1)}, bf16[16,16384]{1,0:T(8,128)(2,1)S(1)}, u32[]{:S(2)}, u32[]{:S(2)}) collective-permute-start(bf16[16,16384]{1,0:T(8,128)(2,1)S(1)} %broadcast_select_fusion.3), channel_id=1, source_target_pairs={{32,0},{40,8},{48,16},{56,24},{64,32},{72,40},{80,48},{88,56},{96,... | collective-permute-start | bytes 1572872 | tf_op jit(solution)/shard_map/ppermute | solution.py:10
  139.0 16.7 %collective-permute-start.3 = (f32[16,16384]{1,0:T(8,128)S(1)}, f32[16,16384]{1,0:T(8,128)S(1)}, u32[]{:S(2)}, u32[]{:S(2)}) collective-permute-start(f32[16,16384]{1,0:T(8,128)S(1)} %copy_bitcast_fusion), channel_id=1, source_target_pairs={{248,0},{0,8},{8,16},{16,24},{24,32},{32,40},{40,48},{48,56},{56,6... | collective-permute-start | bytes 3145736 | tf_op jit(solution)/shard_map/ppermute | solution.py:10
  155.8 66.0 %collective-permute-start.4 = (f32[16,16384]{1,0:T(8,128)S(1)}, f32[16,16384]{1,0:T(8,128)S(1)}, u32[]{:S(2)}, u32[]{:S(2)}) collective-permute-start(f32[16,16384]{1,0:T(8,128)S(1)} %broadcast_select_fusion), channel_id=1, source_target_pairs={{240,0},{248,8},{0,16},{8,24},{16,32},{24,40},{32,48},{40,56},{48,... | collective-permute-start | bytes 3145736 | tf_op jit(solution)/shard_map/ppermute | solution.py:10
  221.9 20.6 %collective-permute-start.5 = (f32[16,16384]{1,0:T(8,128)S(1)}, f32[16,16384]{1,0:T(8,128)S(1)}, u32[]{:S(2)}, u32[]{:S(2)}) collective-permute-start(f32[16,16384]{1,0:T(8,128)S(1)} %broadcast_select_fusion.2), channel_id=1, source_target_pairs={{224,0},{232,8},{240,16},{248,24},{0,32},{8,40},{16,48},{24,56},{3... | collective-permute-start | bytes 3145736 | tf_op jit(solution)/shard_map/ppermute | solution.py:10
Sparse Core Ops, SparseCore 0:
  243.9 49.2 reduce-scatter.1
where the time goes:
time: 302 us; the launch traced here: 300 us
  waiting for transfers between devices  133 us (44%)
  starting transfers between devices  54.7 us (18%)
  blocking collectives  29.6 us (10%)
  other arithmetic  27.9 us (9%)
  matrix products  21.5 us (7%)
  local copies, waits for them, and re-layouts  18.4 us (6%)
  between operations  14.1 us (5%)
    ppermute x6, waiting for transfers between devices, passed_along(): return lax.ppermute(block, axis, route)  83.9 us
    ppermute x6, starting transfers between devices, passed_along(): return lax.ppermute(block, axis, route)  54.7 us
    reduce_scatter x1, waiting for transfers between devices, per_device(): lax.psum_scatter(row_part + carried, 'off', scatter_dimension=1, tiled=True)  49.4 us
    all_gather x1, blocking collectives, per_device(): row_segment = lax.all_gather(vectors, 'off', axis=1, tiled=True)  29.6 us
    dot_general x6, matrix products, one_round(): jnp.einsum('ktj,tij->kti', from_cols, blocks, preferred_element_type=jnp....  11.5 us
    scatter-add x6, other arithmetic, one_round(): row_acc = row_acc.at[:, index_part[:, 0]].add(forward)  10.3 us
    scatter-add x6, other arithmetic, one_round(): col_acc = col_acc.at[:, index_part[:, 1]].add(backward)  10.2 us
    dot_general x6, matrix products, one_round(): jnp.einsum('kti,tij->ktj', from_rows, blocks, preferred_element_type=jnp....  10 us
  transfers between devices with their start and end apart: 7, of which 7 were waited for; matrix products, arithmetic and copies ran while one was open for 0% of the time, Pallas kernels for 0%

commit v1 on v0

v1 whole, which is shorter than its diff:
```python
import functools

import jax
import jax.numpy as jnp
from jax import lax
from jax.experimental import pallas as pl
from jax.experimental.pallas import tpu as pltpu
from jax.sharding import PartitionSpec as P

AXES = ("diag", "off")
TILE = 128
UNROLL = 32
VMEM = pl.BlockSpec(memory_space=pltpu.VMEM)
SMEM = pl.BlockSpec(memory_space=pltpu.SMEM)


def params(mib):
    return pltpu.CompilerParams(vmem_limit_bytes=mib * 2**20)


def block_at(ref, block, per_part):
    lanes = pl.multiple_of(lax.rem(block, per_part) * TILE, TILE)
    return ref.at[lax.div(block, per_part), :, pl.ds(lanes, TILE)]


def quantized(source, target, part, per_part):
    nvecs = source.shape[1]
    lane = lax.broadcasted_iota(jnp.int32, (nvecs, TILE), 1)
    exponents = jnp.zeros((nvecs, TILE), jnp.int32)
    for block in range(per_part):
        values = source[part, :, block * TILE : (block + 1) * TILE]
        largest = jnp.max(jnp.abs(values), axis=1, keepdims=True)
        power = jnp.floor(jnp.log2(jnp.maximum(largest, 2.0**-100)))
        scaled = jnp.round(values * jnp.exp2(14.0 - power))
        scaled = jnp.clip(scaled, -32767.0, 32767.0).astype(jnp.int32)
        target[part, :, block * TILE : (block + 1) * TILE] = scaled.astype(jnp.int16)
        exponents = jnp.where(lane == block, power.astype(jnp.int32), exponents)
    target[part, :, per_part * TILE :] = exponents.astype(jnp.int16)


def restored(source, part, block, per_part):
    exponents = source[part, :, per_part * TILE :].astype(jnp.int32).astype(jnp.float32)
    scale = jnp.exp2(exponents[:, block : block + 1] - 14.0)
    values = source[part, :, block * TILE : (block + 1) * TILE]
    return values.astype(jnp.int32).astype(jnp.float32) * scale


def tiles_kernel(transposed, per_part, meta, count, x_ref, tiles_ref, out_ref, acc_ref=None):
    total = out_ref if acc_ref is None else acc_ref
    live = count[0]
    nvecs = x_ref.shape[1]
    total[...] = jnp.zeros_like(total)
    lane = lax.broadcasted_iota(jnp.int32, (nvecs, TILE), 1)

    def group(index, carry):
        products = []
        for step in range(UNROLL):
            slot = index * UNROLL + step
            code = meta[slot]
            alive = slot < live
            rows = jnp.where(alive, (code >> 14) & 0xFF, 0)
            columns = jnp.where(alive, (code >> 22) & 0xFF, 0)
            row_block, column_block = code & 0x7F, (code >> 7) & 0x7F
            if transposed:
                taken, given, source, target = columns, rows, column_block, row_block
            else:
                taken, given, source, target = rows, columns, row_block, column_block
            x = block_at(x_ref, source, per_part)[...]
            x = jnp.where(lane < taken, x.astype(jnp.float32), 0.0).astype(jnp.bfloat16)
            dims = (((1,), (1 if transposed else 0,)), ((), ()))
            product = lax.dot_general(x, tiles_ref[slot], dims, preferred_element_type=jnp.float32)
            products.append((target, jnp.where(lane < given, product, 0.0)))
        for target, product in products:
            block_at(total, target, per_part)[...] += product
        return carry

    lax.fori_loop(0, lax.div(live + UNROLL - 1, UNROLL), group, 0)
    if acc_ref is not None:
        def part_out(part, carry):
            quantized(acc_ref, out_ref, part, per_part)
            return carry

        lax.fori_loop(0, out_ref.shape[0], part_out, 0)


def column_partials(meta, count, x, tiles):
    parts, nvecs, width = x.shape
    per_part = width // TILE
    return pl.pallas_call(
        functools.partial(tiles_kernel, False, per_part),
        out_shape=jax.ShapeDtypeStruct((parts, nvecs, width + TILE), jnp.int16),
        in_specs=[SMEM, SMEM, VMEM, VMEM],
        out_specs=VMEM,
        scratch_shapes=[pltpu.VMEM((parts, nvecs, width), jnp.float32)],
        compiler_params=params(32),
        cost_estimate=pl.CostEstimate(flops=10**9, bytes_accessed=12 * 2**20, transcendentals=0),
    )(meta, count, x, tiles)


def row_partials(meta, count, x, tiles):
    parts, nvecs, width = x.shape
    per_part = width // TILE
    return pl.pallas_call(
        functools.partial(tiles_kernel, True, per_part),
        out_shape=jax.ShapeDtypeStruct((parts, nvecs, width), jnp.float32),
        in_specs=[SMEM, SMEM, VMEM, VMEM],
        out_specs=VMEM,
        compiler_params=params(32),
        cost_estimate=pl.CostEstimate(flops=10**9, bytes_accessed=12 * 2**20, transcendentals=0),
    )(meta, count, x, tiles)


def joined_kernel(per_part, rows_ref, arrived_ref, out_ref, total_ref):
    def one_part(part, carry):
        for block in range(per_part):
            lanes = slice(block * TILE, (block + 1) * TILE)
            total_ref[part, :, lanes] = rows_ref[part, :, lanes] + restored(arrived_ref, part, block, per_part)
        quantized(total_ref, out_ref, part, per_part)
        return carry

    lax.fori_loop(0, out_ref.shape[0], one_part, 0)


def joined(rows, arrived):
    parts, nvecs, width = rows.shape
    return pl.pallas_call(
        functools.partial(joined_kernel, width // TILE),
        out_shape=jax.ShapeDtypeStruct(arrived.shape, jnp.int16),
        in_specs=[VMEM, VMEM],
        out_specs=VMEM,
        scratch_shapes=[pltpu.VMEM((parts, nvecs, width), jnp.float32)],
        compiler_params=params(16),
    )(rows, arrived)


def summed_kernel(per_part, parts_ref, out_ref):
    for block in range(per_part):
        total = restored(parts_ref, 0, block, per_part)
        for part in range(1, parts_ref.shape[0]):
            total = total + restored(parts_ref, part, block, per_part)
        out_ref[:, block * TILE : (block + 1) * TILE] = total


def summed(parts):
    nvecs, width = parts.shape[1], parts.shape[2] - TILE
    return pl.pallas_call(
        functools.partial(summed_kernel, width // TILE),
        out_shape=jax.ShapeDtypeStruct((nvecs, width), jnp.float32),
        in_specs=[VMEM],
        out_specs=VMEM,
        compiler_params=params(16),
    )(parts)


def per_device(vectors, tile_blocks, tile_index, tile_live, tile_count):
    n_diag, n_off = lax.axis_size("diag"), lax.axis_size("off")
    fetch = [
        (((a + b) % n_diag) * n_off + b, a * n_off + b) for a in range(n_diag) for b in range(n_off)
    ]
    meta = tile_index[:, 0] | (tile_index[:, 1] << 7) | (tile_live[:, 0] << 14) | (tile_live[:, 1] << 22)
    copies = jnp.broadcast_to(vectors[None], (n_off, *vectors.shape))
    x_rows = lax.all_to_all(copies, "off", 0, 0)
    x_columns = lax.ppermute(x_rows, AXES, fetch)
    sent = column_partials(meta, tile_count, x_rows, tile_blocks)
    arrived = lax.ppermute(sent, AXES, [(there, here) for here, there in fetch])
    rows = row_partials(meta, tile_count, x_columns, tile_blocks)
    return summed(lax.all_to_all(joined(rows, arrived), "off", 0, 0))


def solution(mesh):
    placed = (
        P(None, AXES),
        P(AXES, None, None),
        P(AXES, None),
        P(AXES, None),
        P(AXES),
    )
    return jax.shard_map(
        per_device, mesh=mesh, in_specs=placed, out_specs=P(None, AXES), check_vma=False
    )
```

time: 302 us -> 83.1 us (0.28)
  the two profiles are of different devices: /device:TPU:32 before, /device:TPU:2 now
where the time goes in v1:
time: 83.1 us; the launch traced here: 82.6 us
  blocking collectives  33.1 us (40%)
  waiting for transfers between devices  16.7 us (20%)
  starting transfers between devices  16 us (19%)
  Pallas kernels  9.63 us (12%)
  local copies, waits for them, and re-layouts  5.68 us (7%)
    all_to_all x1, blocking collectives, per_device(): return summed(lax.all_to_all(joined(rows, arrived), 'off', 0, 0))  33.1 us
    ppermute x1, waiting for transfers between devices, per_device(): arrived = lax.ppermute(sent, AXES, [(there, here) for here, there in fetch])  9.22 us
    ppermute x1, starting transfers between devices, per_device(): x_columns = lax.ppermute(x_rows, AXES, fetch)  8.2 us
    all_to_all x1, waiting for transfers between devices, per_device(): x_rows = lax.all_to_all(copies, 'off', 0, 0)  7.48 us
    all_to_all x1, starting transfers between devices, per_device(): x_rows = lax.all_to_all(copies, 'off', 0, 0)  5.84 us
    unnamed x4, local copies, waits for them, and re-layouts  4 us
    pallas_call x1, Pallas kernels, column_partials(): pl.pallas_call(functools.partial(tiles_kernel, False, per_part), out_shap...  3.48 us
    pallas_call x1, Pallas kernels, row_partials(): pl.pallas_call(functools.partial(tiles_kernel, True, per_part), out_shape...  3.29 us
  transfers between devices with their start and end apart: 3, of which 2 were waited for; matrix products, arithmetic and copies ran while one was open for 1% of the time, Pallas kernels for 8%

profile of v1, /device:TPU:2, one launch (start us, length us, event | category | flops | bytes accessed | tf_op | source)
XLA Modules:
  0.0 82.6 jit_solution(8726140503353791782)
XLA Ops:
  0.0 1.7 %broadcast_in_dim.2 = bf16[8,16,2048]{2,1,0:T(8,128)(2,1)} broadcast(bf16[16,2048]{1,0:T(8,128)(2,1)} %param.5), dimensions={1,2} | broadcast | bytes 589824 | tf_op jit(solution)/shard_map/broadcast_in_dim | solution.py:161
  1.7 5.8 %all-to-all-start = ((bf16[8,16,2048]{2,1,0:T(8,128)(2,1)}), bf16[8,16,2048]{2,1,0:T(8,128)(2,1)S(1)}, u32[]{:S(2)}, u32[]{:S(2)}) async-start(bf16[8,16,2048]{2,1,0:T(8,128)(2,1)} %broadcast_in_dim.2), calls=%async_computation | async-start | bytes 1048576 | tf_op jit(solution)/shard_map/all_to_all | solution.py:162
  8.2 0.8 or_reduce_fusion.meta
  9.0 7.5 %all-to-all-done.x_ref = bf16[8,16,2048]{2,1,0:T(8,128)(2,1)S(1)} async-done(((bf16[8,16,2048]{2,1,0:T(8,128)(2,1)}), bf16[8,16,2048]{2,1,0:T(8,128)(2,1)S(1)}, u32[]{:S(2)}, u32[]{:S(2)}) %all-to-all-start) | async-done | bytes 524320 | tf_op jit(solution)/shard_map/all_to_all | solution.py:162
  16.4 8.2 %collective-permute-start = (bf16[8,16,2048]{2,1,0:T(8,128)(2,1)S(1)}, bf16[8,16,2048]{2,1,0:T(8,128)(2,1)S(1)}, u32[]{:S(2)}, u32[]{:S(2)}) collective-permute-start(bf16[8,16,2048]{2,1,0:T(8,128)(2,1)S(1)} %all-to-all-done.x_ref), channel_id=1, source_target_pairs={{0,0},{9,1},{18,2},{27,3},{36,4},{45,5},{54,6},{63,7},{8,8},{17,9}... | collective-permute-start | bytes 1572872 | tf_op jit(solution)/shard_map/ppermute | solution.py:163
  24.6 0.0 copy-start
  24.7 4.0 %copy-done = bf16[320,128,128]{2,1,0:T(8,128)(2,1)S(1)} copy-done((bf16[320,128,128]{2,1,0:T(8,128)(2,1)S(1)}, bf16[320,128,128]{2,1,0:T(8,128)(2,1)}, u32[]{:S(2)}) %copy-start) | copy-done | bytes 10485784
  28.6 0.0 copy-start.1
  28.6 3.5 %shard_map.56 = s16[8,16,2176]{2,1,0:T(8,128)(2,1)S(1)} custom-call(s32[320]{0:T(512)S(1)} %or_reduce_fusion.meta, s32[1]{0:T(128)S(6)} %copy.6.count, bf16[8,16,2048]{2,1,0:T(8,128)(2,1)S(1)} %all-to-all-done.x_ref, bf16[320,128,128]{2,1,0:T(8,128)(2,1)S(1)} %copy-done), custom_call_target="tpu_custom_call" | custom-call | flops 1000000000 | bytes 12582912 | tf_op jit(solution)/shard_map/pallas_call | solution.py:89
  32.1 1.9 %collective-permute-start.1 = (s16[8,16,2176]{2,1,0:T(8,128)(2,1)S(1)}, s16[8,16,2176]{2,1,0:T(8,128)(2,1)S(1)}, u32[]{:S(2)}, u32[]{:S(2)}) collective-permute-start(s16[8,16,2176]{2,1,0:T(8,128)(2,1)S(1)} %shard_map.56), channel_id=1, source_target_pairs={{0,0},{1,9},{2,18},{3,27},{4,36},{5,45},{6,54},{7,63},{8,8},{9,17}... | collective-permute-start | bytes 1671176 | tf_op jit(solution)/shard_map/ppermute | solution.py:165
  34.1 0.0 collective-permute-done.x_ref
  34.1 0.0 copy-done.1
  34.1 3.3 %shard_map.55.rows_ref = f32[8,16,2048]{2,1,0:T(8,128)S(1)} custom-call(s32[320]{0:T(512)S(1)} %or_reduce_fusion.meta, s32[1]{0:T(128)S(6)} %copy.6.count, bf16[8,16,2048]{2,1,0:T(8,128)(2,1)S(1)} %collective-permute-done.x_ref, bf16[320,128,128]{2,1,0:T(8,128)(2,1)S(1)} %copy-done.1), custom_call_target="tpu_custom_call" | custom-call | flops 1000000000 | bytes 12582912 | tf_op jit(solution)/shard_map/pallas_call | solution.py:103
  37.4 9.2 %collective-permute-done.1.arrived_ref = s16[8,16,2176]{2,1,0:T(8,128)(2,1)S(1)} collective-permute-done((s16[8,16,2176]{2,1,0:T(8,128)(2,1)S(1)}, s16[8,16,2176]{2,1,0:T(8,128)(2,1)S(1)}, u32[]{:S(2)}, u32[]{:S(2)}) %collective-permute-start.1) | collective-permute-done | bytes 557088 | tf_op jit(solution)/shard_map/ppermute | solution.py:165
  46.6 1.8 %shard_map.57 = s16[8,16,2176]{2,1,0:T(8,128)(2,1)S(1)} custom-call(f32[8,16,2048]{2,1,0:T(8,128)S(1)} %shard_map.55.rows_ref, s16[8,16,2176]{2,1,0:T(8,128)(2,1)S(1)} %collective-permute-done.1.arrived_ref), custom_call_target="tpu_custom_call" | custom-call | tf_op jit(solution)/shard_map/pallas_call | solution.py:126
  48.4 33.1 %all_to_all.10.parts_ref = s16[8,16,2176]{2,1,0:T(8,128)(2,1)S(1)} all-to-all(s16[8,16,2176]{2,1,0:T(8,128)(2,1)S(1)} %shard_map.57), channel_id=1, replica_groups=mesh['diag'=32,'off'=8] {'off'}, dimensions={0} | all-to-all | bytes 1114112 | tf_op jit(solution)/shard_map/all_to_all | solution.py:167
  81.6 1.0 %shard_map.58 = f32[16,2048]{1,0:T(8,128)} custom-call(s16[8,16,2176]{2,1,0:T(8,128)(2,1)S(1)} %all_to_all.10.parts_ref), custom_call_target="tpu_custom_call" | custom-call | tf_op jit(solution)/shard_map/pallas_call | solution.py:146
Async XLA Ops:
  1.7 14.8 %all-to-all-start = ((bf16[8,16,2048]{2,1,0:T(8,128)(2,1)}), bf16[8,16,2048]{2,1,0:T(8,128)(2,1)S(1)}, u32[]{:S(2)}, u32[]{:S(2)}) async-start(bf16[8,16,2048]{2,1,0:T(8,128)(2,1)} %broadcast_in_dim.2), calls=%async_computation | async-start | bytes 1048576 | tf_op jit(solution)/shard_map/all_to_all | solution.py:162
  16.4 17.6 %collective-permute-start = (bf16[8,16,2048]{2,1,0:T(8,128)(2,1)S(1)}, bf16[8,16,2048]{2,1,0:T(8,128)(2,1)S(1)}, u32[]{:S(2)}, u32[]{:S(2)}) collective-permute-start(bf16[8,16,2048]{2,1,0:T(8,128)(2,1)S(1)} %all-to-all-done.x_ref), channel_id=1, source_target_pairs={{0,0},{9,1},{18,2},{27,3},{36,4},{45,5},{54,6},{63,7},{8,8},{17,9}... | collective-permute-start | bytes 1572872 | tf_op jit(solution)/shard_map/ppermute | solution.py:163
  24.6 4.0 %copy-start = (bf16[320,128,128]{2,1,0:T(8,128)(2,1)S(1)}, bf16[320,128,128]{2,1,0:T(8,128)(2,1)}, u32[]{:S(2)}) copy-start(bf16[320,128,128]{2,1,0:T(8,128)(2,1)} %tiles_ref.3) | copy-start | bytes 31457284
  28.6 5.4 %copy-start.1 = (bf16[320,128,128]{2,1,0:T(8,128)(2,1)S(1)}, bf16[320,128,128]{2,1,0:T(8,128)(2,1)}, u32[]{:S(2)}) copy-start(bf16[320,128,128]{2,1,0:T(8,128)(2,1)} %tiles_ref.3) | copy-start | bytes 31457284
  32.1 14.5 %collective-permute-start.1 = (s16[8,16,2176]{2,1,0:T(8,128)(2,1)S(1)}, s16[8,16,2176]{2,1,0:T(8,128)(2,1)S(1)}, u32[]{:S(2)}, u32[]{:S(2)}) collective-permute-start(s16[8,16,2176]{2,1,0:T(8,128)(2,1)S(1)} %shard_map.56), channel_id=1, source_target_pairs={{0,0},{1,9},{2,18},{3,27},{4,36},{5,45},{6,54},{7,63},{8,8},{9,17}... | collective-permute-start | bytes 1671176 | tf_op jit(solution)/shard_map/ppermute | solution.py:165

commit v2 on v1

v2 whole, which is shorter than its diff:
```python
import functools

import jax
import jax.numpy as jnp
from jax import lax
from jax.experimental import pallas as pl
from jax.experimental.pallas import tpu as pltpu
from jax.sharding import PartitionSpec as P

AXES = ("diag", "off")
TILE = 128
UNROLL = 32
VMEM = pl.BlockSpec(memory_space=pltpu.VMEM)
HBM = pl.BlockSpec(memory_space=pltpu.HBM)
SMEM = pl.BlockSpec(memory_space=pltpu.SMEM)


def params(mib):
    return pltpu.CompilerParams(vmem_limit_bytes=mib * 2**20)


def block_at(ref, block, per_part):
    lanes = pl.multiple_of(lax.rem(block, per_part) * TILE, TILE)
    return ref.at[lax.div(block, per_part), :, pl.ds(lanes, TILE)]


def quantized(source, target, part, per_part):
    nvecs = source.shape[1]
    lane = lax.broadcasted_iota(jnp.int32, (nvecs, TILE), 1)
    exponents = jnp.zeros((nvecs, TILE), jnp.int32)
    for block in range(per_part):
        values = source[part, :, block * TILE : (block + 1) * TILE]
        largest = jnp.max(jnp.abs(values), axis=1, keepdims=True)
        power = jnp.floor(jnp.log2(jnp.maximum(largest, 2.0**-100)))
        scaled = jnp.round(values * jnp.exp2(14.0 - power))
        scaled = jnp.clip(scaled, -32767.0, 32767.0).astype(jnp.int32)
        target[part, :, block * TILE : (block + 1) * TILE] = scaled.astype(jnp.int16)
        exponents = jnp.where(lane == block, power.astype(jnp.int32), exponents)
    target[part, :, per_part * TILE :] = exponents.astype(jnp.int16)


def restored(source, part, block, per_part):
    exponents = source[part, :, per_part * TILE :].astype(jnp.int32).astype(jnp.float32)
    scale = jnp.exp2(exponents[:, block : block + 1] - 14.0)
    values = source[part, :, block * TILE : (block + 1) * TILE]
    return values.astype(jnp.int32).astype(jnp.float32) * scale


def tiles_kernel(transposed, per_part, meta, count, x_ref, stored_ref, out_ref, total, tiles_ref, arrived):
    live = count[0]
    groups = lax.div(live + UNROLL - 1, UNROLL)

    def fetched(index):
        part = pl.ds(index * UNROLL, UNROLL)
        return pltpu.make_async_copy(stored_ref.at[part], tiles_ref.at[part], arrived.at[index])

    def start(index, carry):
        fetched(index).start()
        return carry

    lax.fori_loop(0, groups, start, 0)
    nvecs = x_ref.shape[1]
    total[...] = jnp.zeros_like(total)
    lane = lax.broadcasted_iota(jnp.int32, (nvecs, TILE), 1)
    source, target = (1, 0) if transposed else (0, 1)

    def group(index, carry):
        fetched(index).wait()
        products = []
        for step in range(UNROLL):
            slot = index * UNROLL + step
            alive = slot < live
            code = meta[slot]
            blocks = (code & 0x7F, (code >> 7) & 0x7F)
            widths = [jnp.where(alive, (code >> shift) & 0xFF, 0) for shift in (14, 22)]
            taken, given = widths[source], widths[target]
            x = block_at(x_ref, blocks[source], per_part)[...]
            x = jnp.where(lane < taken, x.astype(jnp.float32), 0.0).astype(jnp.bfloat16)
            dims = (((1,), (1 if transposed else 0,)), ((), ()))
            product = lax.dot_general(x, tiles_ref[slot], dims, preferred_element_type=jnp.float32)
            products.append((blocks[target], jnp.where(lane < given, product, 0.0)))
        for block, product in products:
            block_at(total, block, per_part)[...] += product
        return carry

    lax.fori_loop(0, groups, group, 0)

    def part_out(part, carry):
        quantized(total, out_ref, part, per_part)
        return carry

    lax.fori_loop(0, out_ref.shape[0], part_out, 0)


def partials(transposed, meta, count, x, tiles):
    parts, nvecs, width = x.shape
    return pl.pallas_call(
        functools.partial(tiles_kernel, transposed, width // TILE),
        out_shape=jax.ShapeDtypeStruct((parts, nvecs, width + TILE), jnp.int16),
        in_specs=[SMEM, SMEM, VMEM, HBM],
        out_specs=VMEM,
        scratch_shapes=[
            pltpu.VMEM((parts, nvecs, width), jnp.float32),
            pltpu.VMEM(tiles.shape, tiles.dtype),
            pltpu.SemaphoreType.DMA((tiles.shape[0] // UNROLL,)),
        ],
        compiler_params=params(48),
        cost_estimate=pl.CostEstimate(flops=10**9, bytes_accessed=12 * 2**20, transcendentals=0),
    )(meta, count, x, tiles)


column_partials = functools.partial(partials, False)
row_partials = functools.partial(partials, True)


def summed_kernel(per_part, count, *refs):
    out_ref = refs[count]
    total_ref = out_ref if out_ref.dtype == jnp.float32 else refs[count + 1]
    for block in range(per_part):
        terms = [restored(ref, part, block, per_part) for ref in refs[:count] for part in range(ref.shape[0])]
        total = terms[0]
        for term in terms[1:]:
            total = total + term
        total_ref[0, :, block * TILE : (block + 1) * TILE] = total
    if total_ref is not out_ref:
        quantized(total_ref, out_ref, 0, per_part)


def summed(*parts, packed=False):
    _, nvecs, packed_width = parts[0].shape
    width = packed_width - TILE
    shape = (1, nvecs, packed_width if packed else width)
    return pl.pallas_call(
        functools.partial(summed_kernel, width // TILE, len(parts)),
        out_shape=jax.ShapeDtypeStruct(shape, jnp.int16 if packed else jnp.float32),
        in_specs=[VMEM] * len(parts),
        out_specs=VMEM,
        scratch_shapes=[pltpu.VMEM((1, nvecs, width), jnp.float32)] if packed else [],
        compiler_params=params(16),
    )(*parts)


def joined_kernel(per_part, rows_ref, arrived_ref, out_ref, total_ref):
    def one_part(part, carry):
        for block in range(per_part):
            lanes = slice(block * TILE, (block + 1) * TILE)
            total_ref[part, :, lanes] = restored(rows_ref, part, block, per_part) + restored(arrived_ref, part, block, per_part)
        quantized(total_ref, out_ref, part, per_part)
        return carry

    lax.fori_loop(0, out_ref.shape[0], one_part, 0)


def joined(rows, arrived):
    parts, nvecs, width = rows.shape[0], rows.shape[1], rows.shape[2] - TILE
    return pl.pallas_call(
        functools.partial(joined_kernel, width // TILE),
        out_shape=jax.ShapeDtypeStruct(arrived.shape, jnp.int16),
        in_specs=[VMEM, VMEM],
        out_specs=VMEM,
        scratch_shapes=[pltpu.VMEM((parts, nvecs, width), jnp.float32)],
        compiler_params=params(16),
    )(rows, arrived)


def per_device(vectors, tile_blocks, tile_index, tile_live, tile_count):
    n_diag, n_off = lax.axis_size("diag"), lax.axis_size("off")
    at = lambda a, b: (a % n_diag) * n_off + b
    across = lambda a, b: ((a >> 1) ^ ((a + b) >> 1)) & 1
    other = lambda a, b: b ^ (n_off // 2) if across(a, b) else b
    devices = [(a, b) for a in range(n_diag) for b in range(n_off)]
    fetch = [(at(a + b, other(a, b)), at(a, b)) for a, b in devices]
    back = [(at(a, b), at(a + b, (b if (a + b) % 2 == 0 else 7 - b))) for a, b in devices]
    meta = tile_index[:, 0] | (tile_index[:, 1] << 7) | (tile_live[:, 0] << 14) | (tile_live[:, 1] << 22)
    copies = jnp.broadcast_to(vectors[None], (n_off, *vectors.shape))
    copies, meta = lax.optimization_barrier((copies, meta))
    x_rows = lax.all_to_all(copies, "off", 0, 0)
    x_columns = lax.ppermute(x_rows, AXES, fetch)
    columns = column_partials(meta, tile_count, x_rows, tile_blocks)
    arrived = lax.ppermute(columns, AXES, back)
    rows = row_partials(meta, tile_count, x_columns, tile_blocks)
    return summed(lax.all_to_all(joined(rows, arrived), "off", 0, 0))[0]


def solution(mesh):
    placed = (
        P(None, AXES),
        P(AXES, None, None),
        P(AXES, None),
        P(AXES, None),
        P(AXES),
    )
    return jax.shard_map(
        per_device, mesh=mesh, in_specs=placed, out_specs=P(None, AXES), check_vma=False
    )
```

time: 83.1 us -> 75.7 us (0.911)
  the two profiles are of different devices: /device:TPU:2 before, /device:TPU:33 now
where the time goes in v2:
time: 75.7 us; the launch traced here: 75.4 us
  waiting for transfers between devices  33.4 us (44%)
  Pallas kernels  15.8 us (21%)
  blocking collectives  13 us (17%)
  starting transfers between devices  9.99 us (13%)
  local copies, waits for them, and re-layouts  1.67 us (2%)
  other arithmetic  0.79 us (1%)
    ppermute x1, waiting for transfers between devices, per_device(): arrived = lax.ppermute(columns, AXES, back)  23.9 us
    all_to_all x1, blocking collectives, per_device(): return summed(lax.all_to_all(joined(rows, arrived), 'off', 0, 0))[0]  13 us
    pallas_call x2, Pallas kernels, partials(): pl.pallas_call(functools.partial(tiles_kernel, transposed, width // TILE)...  12.7 us
    all_to_all x1, waiting for transfers between devices, per_device(): x_rows = lax.all_to_all(copies, 'off', 0, 0)  9.54 us
    all_to_all x1, starting transfers between devices, per_device(): x_rows = lax.all_to_all(copies, 'off', 0, 0)  5.03 us
    ppermute x1, starting transfers between devices, per_device(): arrived = lax.ppermute(columns, AXES, back)  4.28 us
    pallas_call x1, Pallas kernels, joined(): pl.pallas_call(functools.partial(joined_kernel, width // TILE), out_shape...  2.11 us
    broadcast_in_dim x1, local copies, waits for them, and re-layouts, per_device(): copies = jnp.broadcast_to(vectors[None], (n_off, *vectors.shape))  1.67 us
  transfers between devices with their start and end apart: 3, of which 2 were waited for; matrix products, arithmetic and copies ran while one was open for 0% of the time, Pallas kernels for 17%

profile of v2, /device:TPU:33, one launch (start us, length us, event | category | flops | bytes accessed | tf_op | source)
XLA Modules:
  0.0 75.4 jit_solution(7246020107619664607)
XLA Ops:
  0.0 0.8 %or_reduce_fusion.meta = s32[320]{0:T(512)S(1)} fusion(s32[320,2]{0,1:T(2,128)} %param.8, s32[320,2]{0,1:T(2,128)} %param.7), kind=kLoop, calls=%fused_computation | loop fusion | flops 1920 | bytes 6400 | tf_op jit(solution)/shard_map/or | solution.py:174
  0.8 1.7 %broadcast_in_dim.2 = bf16[8,16,2048]{2,1,0:T(8,128)(2,1)} broadcast(bf16[16,2048]{1,0:T(8,128)(2,1)} %param.5), dimensions={1,2} | broadcast | bytes 589824 | tf_op jit(solution)/shard_map/broadcast_in_dim | solution.py:175
  2.5 5.0 %all-to-all-start = ((bf16[8,16,2048]{2,1,0:T(8,128)(2,1)}), bf16[8,16,2048]{2,1,0:T(8,128)(2,1)S(1)}, u32[]{:S(2)}, u32[]{:S(2)}) async-start(bf16[8,16,2048]{2,1,0:T(8,128)(2,1)} %broadcast_in_dim.2), calls=%async_computation | async-start | bytes 1048576 | tf_op jit(solution)/shard_map/all_to_all | solution.py:177
  8.1 9.5 %all-to-all-done.x_ref = bf16[8,16,2048]{2,1,0:T(8,128)(2,1)S(1)} async-done(((bf16[8,16,2048]{2,1,0:T(8,128)(2,1)}), bf16[8,16,2048]{2,1,0:T(8,128)(2,1)S(1)}, u32[]{:S(2)}, u32[]{:S(2)}) %all-to-all-start) | async-done | bytes 524320 | tf_op jit(solution)/shard_map/all_to_all | solution.py:177
  17.7 0.7 collective-permute-start
  18.4 5.7 %shard_map.56 = s16[8,16,2176]{2,1,0:T(8,128)(2,1)S(1)} custom-call(s32[320]{0:T(512)S(1)} %or_reduce_fusion.meta, s32[1]{0:T(128)S(6)} %copy.6.count, bf16[8,16,2048]{2,1,0:T(8,128)(2,1)S(1)} %all-to-all-done.x_ref, bf16[320,128,128]{2,1,0:T(8,128)(2,1)} %stored_ref.3), custom_call_target="tpu_custom_call" | custom-call | flops 1000000000 | bytes 12582912 | tf_op jit(solution)/shard_map/pallas_call | solution.py:97
  24.0 4.3 %collective-permute-start.1 = (s16[8,16,2176]{2,1,0:T(8,128)(2,1)S(1)}, s16[8,16,2176]{2,1,0:T(8,128)(2,1)S(1)}, u32[]{:S(2)}, u32[]{:S(2)}) collective-permute-start(s16[8,16,2176]{2,1,0:T(8,128)(2,1)S(1)} %shard_map.56), channel_id=1, source_target_pairs={{0,0},{1,14},{2,18},{3,28},{4,36},{5,42},{6,54},{7,56},{8,15},{9,1... | collective-permute-start | bytes 1671176 | tf_op jit(solution)/shard_map/ppermute | solution.py:180
  28.3 0.0 collective-permute-done.x_ref
  28.3 7.0 %shard_map.55.rows_ref = s16[8,16,2176]{2,1,0:T(8,128)(2,1)S(1)} custom-call(s32[320]{0:T(512)S(1)} %or_reduce_fusion.meta, s32[1]{0:T(128)S(6)} %copy.6.count, bf16[8,16,2048]{2,1,0:T(8,128)(2,1)S(1)} %collective-permute-done.x_ref, bf16[320,128,128]{2,1,0:T(8,128)(2,1)} %stored_ref.3), custom_call_target="tpu_custom_call" | custom-call | flops 1000000000 | bytes 12582912 | tf_op jit(solution)/shard_map/pallas_call | solution.py:97
  35.4 23.9 %collective-permute-done.1.arrived_ref = s16[8,16,2176]{2,1,0:T(8,128)(2,1)S(1)} collective-permute-done((s16[8,16,2176]{2,1,0:T(8,128)(2,1)S(1)}, s16[8,16,2176]{2,1,0:T(8,128)(2,1)S(1)}, u32[]{:S(2)}, u32[]{:S(2)}) %collective-permute-start.1) | collective-permute-done | bytes 557088 | tf_op jit(solution)/shard_map/ppermute | solution.py:180
  59.2 2.1 %shard_map.57 = s16[8,16,2176]{2,1,0:T(8,128)(2,1)S(1)} custom-call(s16[8,16,2176]{2,1,0:T(8,128)(2,1)S(1)} %shard_map.55.rows_ref, s16[8,16,2176]{2,1,0:T(8,128)(2,1)S(1)} %collective-permute-done.1.arrived_ref), custom_call_target="tpu_custom_call" | custom-call | tf_op jit(solution)/shard_map/pallas_call | solution.py:156
  61.3 13.0 %all_to_all.10.refs_0_ = s16[8,16,2176]{2,1,0:T(8,128)(2,1)S(1)} all-to-all(s16[8,16,2176]{2,1,0:T(8,128)(2,1)S(1)} %shard_map.57), channel_id=1, replica_groups=mesh['diag'=32,'off'=8] {'off'}, dimensions={0} | all-to-all | bytes 1114112 | tf_op jit(solution)/shard_map/all_to_all | solution.py:182
  74.3 1.0 %shard_map.58 = f32[1,16,2048]{2,1,0:T(8,128)} custom-call(s16[8,16,2176]{2,1,0:T(8,128)(2,1)S(1)} %all_to_all.10.refs_0_), custom_call_target="tpu_custom_call" | custom-call | tf_op jit(solution)/shard_map/pallas_call | solution.py:133
Async XLA Ops:
  2.5 15.2 %all-to-all-start = ((bf16[8,16,2048]{2,1,0:T(8,128)(2,1)}), bf16[8,16,2048]{2,1,0:T(8,128)(2,1)S(1)}, u32[]{:S(2)}, u32[]{:S(2)}) async-start(bf16[8,16,2048]{2,1,0:T(8,128)(2,1)} %broadcast_in_dim.2), calls=%async_computation | async-start | bytes 1048576 | tf_op jit(solution)/shard_map/all_to_all | solution.py:177
  17.7 10.6 %collective-permute-start = (bf16[8,16,2048]{2,1,0:T(8,128)(2,1)S(1)}, bf16[8,16,2048]{2,1,0:T(8,128)(2,1)S(1)}, u32[]{:S(2)}, u32[]{:S(2)}) collective-permute-start(bf16[8,16,2048]{2,1,0:T(8,128)(2,1)S(1)} %all-to-all-done.x_ref), channel_id=1, source_target_pairs={{0,0},{9,1},{22,2},{31,3},{36,4},{45,5},{50,6},{59,7},{8,8},{21,9}... | collective-permute-start | bytes 1572872 | tf_op jit(solution)/shard_map/ppermute | solution.py:178
  24.0 35.2 %collective-permute-start.1 = (s16[8,16,2176]{2,1,0:T(8,128)(2,1)S(1)}, s16[8,16,2176]{2,1,0:T(8,128)(2,1)S(1)}, u32[]{:S(2)}, u32[]{:S(2)}) collective-permute-start(s16[8,16,2176]{2,1,0:T(8,128)(2,1)S(1)} %shard_map.56), channel_id=1, source_target_pairs={{0,0},{1,14},{2,18},{3,28},{4,36},{5,42},{6,54},{7,56},{8,15},{9,1... | collective-permute-start | bytes 1671176 | tf_op jit(solution)/shard_map/ppermute | solution.py:180

commit v3 on v2

--- a/solution.py
+++ b/solution.py
@@ -31,7 +31,7 @@
     for block in range(per_part):
         values = source[part, :, block * TILE : (block + 1) * TILE]
         largest = jnp.max(jnp.abs(values), axis=1, keepdims=True)
-        power = jnp.floor(jnp.log2(jnp.maximum(largest, 2.0**-100)))
+        power = jnp.floor(jnp.log2(jnp.maximum(largest, 2.0**-112)))
         scaled = jnp.round(values * jnp.exp2(14.0 - power))
         scaled = jnp.clip(scaled, -32767.0, 32767.0).astype(jnp.int32)
         target[part, :, block * TILE : (block + 1) * TILE] = scaled.astype(jnp.int16)
@@ -39,14 +39,17 @@
     target[part, :, per_part * TILE :] = exponents.astype(jnp.int16)
 
 
-def restored(source, part, block, per_part):
-    exponents = source[part, :, per_part * TILE :].astype(jnp.int32).astype(jnp.float32)
-    scale = jnp.exp2(exponents[:, block : block + 1] - 14.0)
+def scales_of(source, part, per_part):
+    return jnp.exp2(source[part, :, per_part * TILE :].astype(jnp.int32).astype(jnp.float32) - 14.0)
+
+
+def restored(source, scales, part, block):
     values = source[part, :, block * TILE : (block + 1) * TILE]
-    return values.astype(jnp.int32).astype(jnp.float32) * scale
-
-
-def tiles_kernel(transposed, per_part, meta, count, x_ref, stored_ref, out_ref, total, tiles_ref, arrived):
+    return values.astype(jnp.int32).astype(jnp.float32) * scales[:, block : block + 1]
+
+
+def tiles_kernel(transposed, per_part, pieces, meta, count, x_ref, stored_ref, *refs):
+    sent_refs, (total, tiles_ref, arrived) = refs[:pieces], refs[pieces:]
     live = count[0]
     groups = lax.div(live + UNROLL - 1, UNROLL)
 
@@ -84,23 +87,31 @@
         return carry
 
     lax.fori_loop(0, groups, group, 0)
-
-    def part_out(part, carry):
-        quantized(total, out_ref, part, per_part)
-        return carry
-
-    lax.fori_loop(0, out_ref.shape[0], part_out, 0)
-
-
-def partials(transposed, meta, count, x, tiles):
+    if sent_refs:
+        count_sent = total.shape[0] // len(sent_refs)
+        for first, sent_ref in enumerate(sent_refs):
+
+            def part_out(part, carry):
+                quantized(total.at[pl.ds(first * count_sent, count_sent)], sent_ref, part, per_part)
+                return carry
+
+            lax.fori_loop(0, count_sent, part_out, 0)
+
+
+def partials(transposed, pieces, meta, count, x, tiles):
     parts, nvecs, width = x.shape
+    total = (parts, nvecs, width)
+    if pieces:
+        out_shape = [jax.ShapeDtypeStruct((parts // pieces, nvecs, width + TILE), jnp.int16)] * pieces
+    else:
+        out_shape = [jax.ShapeDtypeStruct(total, jnp.float32)]
     return pl.pallas_call(
-        functools.partial(tiles_kernel, transposed, width // TILE),
-        out_shape=jax.ShapeDtypeStruct((parts, nvecs, width + TILE), jnp.int16),
+        functools.partial(tiles_kernel, transposed, width // TILE, pieces),
+        out_shape=out_shape,
         in_specs=[SMEM, SMEM, VMEM, HBM],
-        out_specs=VMEM,
-        scratch_shapes=[
-            pltpu.VMEM((parts, nvecs, width), jnp.float32),
+        out_specs=[VMEM] * len(out_shape),
+        scratch_shapes=[pltpu.VMEM(total, jnp.float32)] * (1 if pieces else 0)
+        + [
             pltpu.VMEM(tiles.shape, tiles.dtype),
             pltpu.SemaphoreType.DMA((tiles.shape[0] // UNROLL,)),
         ],
@@ -109,15 +120,12 @@
     )(meta, count, x, tiles)
 
 
-column_partials = functools.partial(partials, False)
-row_partials = functools.partial(partials, True)
-
-
 def summed_kernel(per_part, count, *refs):
     out_ref = refs[count]
     total_ref = out_ref if out_ref.dtype == jnp.float32 else refs[count + 1]
+    parts = [(ref, scales_of(ref, part, per_part), part) for ref in refs[:count] for part in range(ref.shape[0])]
     for block in range(per_part):
-        terms = [restored(ref, part, block, per_part) for ref in refs[:count] for part in range(ref.shape[0])]
+        terms = [restored(ref, scales, part, block) for ref, scales, part in parts]
         total = terms[0]
         for term in terms[1:]:
             total = total + term
@@ -140,46 +148,54 @@
     )(*parts)
 
 
-def joined_kernel(per_part, rows_ref, arrived_ref, out_ref, total_ref):
-    def one_part(part, carry):
-        for block in range(per_part):
-            lanes = slice(block * TILE, (block + 1) * TILE)
-            total_ref[part, :, lanes] = restored(rows_ref, part, block, per_part) + restored(arrived_ref, part, block, per_part)
-        quantized(total_ref, out_ref, part, per_part)
-        return carry
-
-    lax.fori_loop(0, out_ref.shape[0], one_part, 0)
-
-
-def joined(rows, arrived):
-    parts, nvecs, width = rows.shape[0], rows.shape[1], rows.shape[2] - TILE
+def joined_kernel(per_part, rows_ref, *refs):
+    arrived_refs, out_ref, total_ref = refs[:-2], refs[-2], refs[-1]
+    each = arrived_refs[0].shape[0]
+    for first, arrived_ref in enumerate(arrived_refs):
+
+        def one_part(part, carry):
+            whole = first * each + part
+            scales = scales_of(arrived_ref, part, per_part)
+            for block in range(per_part):
+                lanes = slice(block * TILE, (block + 1) * TILE)
+                total_ref[whole, :, lanes] = rows_ref[whole, :, lanes] + restored(arrived_ref, scales, part, block)
+            quantized(total_ref, out_ref, whole, per_part)
+            return carry
+
+        lax.fori_loop(0, each, one_part, 0)
+
+
+def joined(rows, *arrived):
+    parts, nvecs, width = rows.shape
     return pl.pallas_call(
         functools.partial(joined_kernel, width // TILE),
-        out_shape=jax.ShapeDtypeStruct(arrived.shape, jnp.int16),
-        in_specs=[VMEM, VMEM],
+        out_shape=jax.ShapeDtypeStruct((parts, nvecs, width + TILE), jnp.int16),
+        in_specs=[VMEM] * (1 + len(arrived)),
         out_specs=VMEM,
         scratch_shapes=[pltpu.VMEM((parts, nvecs, width), jnp.float32)],
         compiler_params=params(16),
-    )(rows, arrived)
+    )(rows, *arrived)
 
 
 def per_device(vectors, tile_blocks, tile_index, tile_live, tile_count):
     n_diag, n_off = lax.axis_size("diag"), lax.axis_size("off")
     at = lambda a, b: (a % n_diag) * n_off + b
     across = lambda a, b: ((a >> 1) ^ ((a + b) >> 1)) & 1
-    other = lambda a, b: b ^ (n_off // 2) if across(a, b) else b
     devices = [(a, b) for a in range(n_diag) for b in range(n_off)]
-    fetch = [(at(a + b, other(a, b)), at(a, b)) for a, b in devices]
-    back = [(at(a, b), at(a + b, (b if (a + b) % 2 == 0 else 7 - b))) for a, b in devices]
+    fetch = [(at(a + b, b ^ (n_off // 2) if across(a, b) else b), at(a, b)) for a, b in devices]
+    homes = [lambda c, b: b ^ 6, lambda c, b: b]
+    copies = jnp.broadcast_to(vectors[None], (n_off, *vectors.shape))
+    x_rows = lax.all_to_all(copies, "off", 0, 0)
+    x_rows, tile_index, tile_live = lax.optimization_barrier((x_rows, tile_index, tile_live))
     meta = tile_index[:, 0] | (tile_index[:, 1] << 7) | (tile_live[:, 0] << 14) | (tile_live[:, 1] << 22)
-    copies = jnp.broadcast_to(vectors[None], (n_off, *vectors.shape))
-    copies, meta = lax.optimization_barrier((copies, meta))
-    x_rows = lax.all_to_all(copies, "off", 0, 0)
     x_columns = lax.ppermute(x_rows, AXES, fetch)
-    columns = column_partials(meta, tile_count, x_rows, tile_blocks)
-    arrived = lax.ppermute(columns, AXES, back)
-    rows = row_partials(meta, tile_count, x_columns, tile_blocks)
-    return summed(lax.all_to_all(joined(rows, arrived), "off", 0, 0))[0]
+    columns = partials(False, len(homes), meta, tile_count, x_rows, tile_blocks)
+    arrived = [
+        lax.ppermute(piece, AXES, [(at(a, b), at(a + b, home(a + b, b))) for a, b in devices])
+        for piece, home in zip(columns, homes)
+    ]
+    (rows,) = partials(True, 0, meta, tile_count, x_columns, tile_blocks)
+    return summed(lax.all_to_all(joined(rows, *arrived), "off", 0, 0))[0]
 
 
 def solution(mesh):

time: 75.7 us -> 72.9 us (0.963)
  blocking collectives: 13 us -> 33.1 us
  waiting for transfers between devices: 33.4 us -> 18.1 us
  starting transfers between devices: 9.99 us -> 2.13 us
  Pallas kernels: 15.8 us -> 16.6 us
  local copies, waits for them, and re-layouts: 1.67 us -> 0.88 us
    all_to_all x1 -> x2, blocking collectives: 13 us -> 33.1 us  [the longest x1 19.1 us: per_device(): return summed(lax.all_to_all(joined(rows, *arrived), 'off', 0, 0))[0]]
    all_to_all x1 -> x0, waiting for transfers between devices: 9.54 us -> none  [per_device(): x_rows = lax.all_to_all(copies, 'off', 0, 0)]
    ppermute x1 -> x2, waiting for transfers between devices: 23.9 us -> 18.1 us  [per_device(): lax.ppermute(piece, AXES, [(at(a, b), at(a + b, home(a + b, b))) for a, b...]
    all_to_all x1 -> x0, starting transfers between devices: 5.03 us -> none  [per_device(): x_rows = lax.all_to_all(copies, 'off', 0, 0)]
    ppermute x1 -> x2, starting transfers between devices: 4.28 us -> 1.45 us  [per_device(): lax.ppermute(piece, AXES, [(at(a, b), at(a + b, home(a + b, b))) for a, b...]
    pallas_call x2, Pallas kernels: 12.7 us -> 13.7 us  [partials(): pl.pallas_call(functools.partial(tiles_kernel, transposed, width // TILE,...]
    broadcast_in_dim x1, local copies, waits for them, and re-layouts: 1.67 us -> 0.88 us  [per_device(): copies = jnp.broadcast_to(vectors[None], (n_off, *vectors.shape))]
  transfers between devices with their start and end apart: 3 -> 3, of which waited for: 2 -> 1; matrix products, arithmetic and copies ran while one was open for 0% -> 1% of each run, Pallas kernels for 17% -> 19%
where the time goes in v3:
time: 72.9 us; the launch traced here: 72.2 us
  blocking collectives  33.1 us (45%)
  waiting for transfers between devices  18.1 us (25%)
  Pallas kernels  16.6 us (23%)
  starting transfers between devices  2.13 us (3%)
  local copies, waits for them, and re-layouts  0.88 us (1%)
  other arithmetic  0.79 us (1%)
    all_to_all x1, blocking collectives, per_device(): return summed(lax.all_to_all(joined(rows, *arrived), 'off', 0, 0))[0]  19.1 us
    ppermute x2, waiting for transfers between devices, per_device(): lax.ppermute(piece, AXES, [(at(a, b), at(a + b, home(a + b, b))) for a, b...  18.1 us
    all_to_all x1, blocking collectives, per_device(): x_rows = lax.all_to_all(copies, 'off', 0, 0)  14 us
    pallas_call x2, Pallas kernels, partials(): pl.pallas_call(functools.partial(tiles_kernel, transposed, width // TILE,...  13.7 us
    pallas_call x1, Pallas kernels, joined(): pl.pallas_call(functools.partial(joined_kernel, width // TILE), out_shape...  1.83 us
  transfers between devices with their start and end apart: 3, of which 1 were waited for; matrix products, arithmetic and copies ran while one was open for 1% of the time, Pallas kernels for 19%

profile of v3, /device:TPU:33, one launch (start us, length us, event | category | flops | bytes accessed | tf_op | source)
XLA Modules:
  0.0 72.2 jit_solution(9388722871175579116)
XLA Ops:
  0.0 0.9 %broadcast_in_dim.2 = bf16[8,16,2048]{2,1,0:T(8,128)(2,1)S(1)} broadcast(bf16[16,2048]{1,0:T(8,128)(2,1)} %param.5), dimensions={1,2} | broadcast | bytes 589824 | tf_op jit(solution)/shard_map/broadcast_in_dim | solution.py:187
  0.9 14.0 %all_to_all.10.x_ref = bf16[8,16,2048]{2,1,0:T(8,128)(2,1)S(1)} all-to-all(bf16[8,16,2048]{2,1,0:T(8,128)(2,1)S(1)} %broadcast_in_dim.2), channel_id=1, replica_groups=mesh['diag'=32,'off'=8] {'off'}, dimensions={0} | all-to-all | bytes 1048576 | tf_op jit(solution)/shard_map/all_to_all | solution.py:188
  14.9 0.7 collective-permute-start
  16.2 0.8 %or_reduce_fusion.meta = s32[320]{0:T(512)S(1)} fusion(s32[320,2]{0,1:T(2,128)} %param.8, s32[320,2]{0,1:T(2,128)} %param.7), kind=kLoop, calls=%fused_computation | loop fusion | flops 1920 | bytes 6400 | tf_op jit(solution)/shard_map/or | solution.py:190
  17.0 6.5 %shard_map.56 = (s16[4,16,2176]{2,1,0:T(8,128)(2,1)S(1)}, s16[4,16,2176]{2,1,0:T(8,128)(2,1)S(1)}) custom-call(s32[320]{0:T(512)S(1)} %or_reduce_fusion.meta, s32[1]{0:T(128)S(6)} %copy.6.count, bf16[8,16,2048]{2,1,0:T(8,128)(2,1)S(1)} %all_to_all.10.x_ref, bf16[320,128,128]{2,1,0:T(8,128)(2,1)} %stored_ref.3), custom_call_target="tpu_custom_call" | custom-call | flops 1000000000 | bytes 12582912 | tf_op jit(solution)/shard_map/pallas_call | solution.py:108
  23.5 0.8 %collective-permute-start.1 = (s16[4,16,2176]{2,1,0:T(8,128)(2,1)S(1)}, s16[4,16,2176]{2,1,0:T(8,128)(2,1)S(1)}, u32[]{:S(2)}, u32[]{:S(2)}) collective-permute-start(s16[4,16,2176]{2,1,0:T(8,128)(2,1)S(1)} %get-tuple-element.13), channel_id=1, source_target_pairs={{0,6},{1,15},{2,20},{3,29},{4,34},{5,43},{6,48},{7,57},{8,14},{9,2... | collective-permute-start | bytes 835592 | tf_op jit(solution)/shard_map/ppermute | solution.py:194
  24.3 0.7 collective-permute-start.2
  25.0 0.0 collective-permute-done.x_ref
  25.0 7.2 %shard_map.55.rows_ref = f32[8,16,2048]{2,1,0:T(8,128)S(1)} custom-call(s32[320]{0:T(512)S(1)} %or_reduce_fusion.meta, s32[1]{0:T(128)S(6)} %copy.6.count, bf16[8,16,2048]{2,1,0:T(8,128)(2,1)S(1)} %collective-permute-done.x_ref, bf16[320,128,128]{2,1,0:T(8,128)(2,1)} %stored_ref.3), custom_call_target="tpu_custom_call" | custom-call | flops 1000000000 | bytes 12582912 | tf_op jit(solution)/shard_map/pallas_call | solution.py:108
  32.2 18.1 %collective-permute-done.1.refs_0_ = s16[4,16,2176]{2,1,0:T(8,128)(2,1)S(1)} collective-permute-done((s16[4,16,2176]{2,1,0:T(8,128)(2,1)S(1)}, s16[4,16,2176]{2,1,0:T(8,128)(2,1)S(1)}, u32[]{:S(2)}, u32[]{:S(2)}) %collective-permute-start.1) | collective-permute-done | bytes 278560 | tf_op jit(solution)/shard_map/ppermute | solution.py:194
  50.3 0.0 collective-permute-done.2.refs_1_
  50.3 1.8 %shard_map.57 = s16[8,16,2176]{2,1,0:T(8,128)(2,1)S(1)} custom-call(f32[8,16,2048]{2,1,0:T(8,128)S(1)} %shard_map.55.rows_ref, s16[4,16,2176]{2,1,0:T(8,128)(2,1)S(1)} %collective-permute-done.1.refs_0_, s16[4,16,2176]{2,1,0:T(8,128)(2,1)S(1)} %collective-permute-done.2.refs_1_), custom_call_target="tpu_custom_call" | custom-call | tf_op jit(solution)/shard_map/pallas_call | solution.py:170
  52.1 19.1 %all_to_all.11.refs_0_ = s16[8,16,2176]{2,1,0:T(8,128)(2,1)S(1)} all-to-all(s16[8,16,2176]{2,1,0:T(8,128)(2,1)S(1)} %shard_map.57), channel_id=1, replica_groups=mesh['diag'=32,'off'=8] {'off'}, dimensions={0} | all-to-all | bytes 1114112 | tf_op jit(solution)/shard_map/all_to_all | solution.py:198
  71.2 1.0 %shard_map.58 = f32[1,16,2048]{2,1,0:T(8,128)} custom-call(s16[8,16,2176]{2,1,0:T(8,128)(2,1)S(1)} %all_to_all.11.refs_0_), custom_call_target="tpu_custom_call" | custom-call | tf_op jit(solution)/shard_map/pallas_call | solution.py:141
Async XLA Ops:
  14.9 10.1 %collective-permute-start = (bf16[8,16,2048]{2,1,0:T(8,128)(2,1)S(1)}, bf16[8,16,2048]{2,1,0:T(8,128)(2,1)S(1)}, u32[]{:S(2)}, u32[]{:S(2)}) collective-permute-start(bf16[8,16,2048]{2,1,0:T(8,128)(2,1)S(1)} %all_to_all.10.x_ref), channel_id=1, source_target_pairs={{0,0},{9,1},{22,2},{31,3},{36,4},{45,5},{50,6},{59,7},{8,8},{21,9}... | collective-permute-start | bytes 1572872 | tf_op jit(solution)/shard_map/ppermute | solution.py:191
  23.5 26.8 %collective-permute-start.1 = (s16[4,16,2176]{2,1,0:T(8,128)(2,1)S(1)}, s16[4,16,2176]{2,1,0:T(8,128)(2,1)S(1)}, u32[]{:S(2)}, u32[]{:S(2)}) collective-permute-start(s16[4,16,2176]{2,1,0:T(8,128)(2,1)S(1)} %get-tuple-element.13), channel_id=1, source_target_pairs={{0,6},{1,15},{2,20},{3,29},{4,34},{5,43},{6,48},{7,57},{8,14},{9,2... | collective-permute-start | bytes 835592 | tf_op jit(solution)/shard_map/ppermute | solution.py:194
  24.3 26.0 %collective-permute-start.2 = (s16[4,16,2176]{2,1,0:T(8,128)(2,1)S(1)}, s16[4,16,2176]{2,1,0:T(8,128)(2,1)S(1)}, u32[]{:S(2)}, u32[]{:S(2)}) collective-permute-start(s16[4,16,2176]{2,1,0:T(8,128)(2,1)S(1)} %get-tuple-element.14), channel_id=1, source_target_pairs={{0,0},{1,9},{2,18},{3,27},{4,36},{5,45},{6,54},{7,63},{8,8},{9,17}... | collective-permute-start | bytes 835592 | tf_op jit(solution)/shard_map/ppermute | solution.py:194

commit v4 on v3

--- a/solution.py
+++ b/solution.py
@@ -183,7 +183,7 @@
     across = lambda a, b: ((a >> 1) ^ ((a + b) >> 1)) & 1
     devices = [(a, b) for a in range(n_diag) for b in range(n_off)]
     fetch = [(at(a + b, b ^ (n_off // 2) if across(a, b) else b), at(a, b)) for a, b in devices]
-    homes = [lambda c, b: b ^ 6, lambda c, b: b]
+    homes = [lambda c, b: b ^ 6, lambda c, b: b ^ 4]
     copies = jnp.broadcast_to(vectors[None], (n_off, *vectors.shape))
     x_rows = lax.all_to_all(copies, "off", 0, 0)
     x_rows, tile_index, tile_live = lax.optimization_barrier((x_rows, tile_index, tile_live))

time: 72.9 us -> 73.7 us (1.011)
  the two profiles are of different devices: /device:TPU:33 before, /device:TPU:129 now
where the time goes in v4:
time: 73.7 us; the launch traced here: 72.7 us
  blocking collectives  37 us (50%)
  Pallas kernels  15.5 us (21%)
  waiting for transfers between devices  12.9 us (18%)
  starting transfers between devices  5.03 us (7%)
  local copies, waits for them, and re-layouts  0.88 us (1%)
  other arithmetic  0.79 us (1%)
    all_to_all x1, blocking collectives, per_device(): return summed(lax.all_to_all(joined(rows, *arrived), 'off', 0, 0))[0]  23 us
    all_to_all x1, blocking collectives, per_device(): x_rows = lax.all_to_all(copies, 'off', 0, 0)  14 us
    ppermute x2, waiting for transfers between devices, per_device(): lax.ppermute(piece, AXES, [(at(a, b), at(a + b, home(a + b, b))) for a, b...  12.9 us
    pallas_call x2, Pallas kernels, partials(): pl.pallas_call(functools.partial(tiles_kernel, transposed, width // TILE,...  12.6 us
    ppermute x2, starting transfers between devices, per_device(): lax.ppermute(piece, AXES, [(at(a, b), at(a + b, home(a + b, b))) for a, b...  4.34 us
    pallas_call x1, Pallas kernels, joined(): pl.pallas_call(functools.partial(joined_kernel, width // TILE), out_shape...  1.83 us
  transfers between devices with their start and end apart: 3, of which 1 were waited for; matrix products, arithmetic and copies ran while one was open for 1% of the time, Pallas kernels for 17%

profile of v4, /device:TPU:129, one launch (start us, length us, event | category | flops | bytes accessed | tf_op | source)
XLA Modules:
  0.0 72.7 jit_solution(5249483409910412247)
XLA Ops:
  0.0 0.9 %broadcast_in_dim.2 = bf16[8,16,2048]{2,1,0:T(8,128)(2,1)S(1)} broadcast(bf16[16,2048]{1,0:T(8,128)(2,1)} %param.5), dimensions={1,2} | broadcast | bytes 589824 | tf_op jit(solution)/shard_map/broadcast_in_dim | solution.py:187
  0.9 14.0 %all_to_all.10.x_ref = bf16[8,16,2048]{2,1,0:T(8,128)(2,1)S(1)} all-to-all(bf16[8,16,2048]{2,1,0:T(8,128)(2,1)S(1)} %broadcast_in_dim.2), channel_id=1, replica_groups=mesh['diag'=32,'off'=8] {'off'}, dimensions={0} | all-to-all | bytes 1048576 | tf_op jit(solution)/shard_map/all_to_all | solution.py:188
  14.9 0.7 collective-permute-start
  16.2 0.8 %or_reduce_fusion.meta = s32[320]{0:T(512)S(1)} fusion(s32[320,2]{0,1:T(2,128)} %param.8, s32[320,2]{0,1:T(2,128)} %param.7), kind=kLoop, calls=%fused_computation | loop fusion | flops 1920 | bytes 6400 | tf_op jit(solution)/shard_map/or | solution.py:190
  17.0 6.1 %shard_map.56 = (s16[4,16,2176]{2,1,0:T(8,128)(2,1)S(1)}, s16[4,16,2176]{2,1,0:T(8,128)(2,1)S(1)}) custom-call(s32[320]{0:T(512)S(1)} %or_reduce_fusion.meta, s32[1]{0:T(128)S(6)} %copy.6.count, bf16[8,16,2048]{2,1,0:T(8,128)(2,1)S(1)} %all_to_all.10.x_ref, bf16[320,128,128]{2,1,0:T(8,128)(2,1)} %stored_ref.3), custom_call_target="tpu_custom_call" | custom-call | flops 1000000000 | bytes 12582912 | tf_op jit(solution)/shard_map/pallas_call | solution.py:108
  23.1 1.2 %collective-permute-start.1 = (s16[4,16,2176]{2,1,0:T(8,128)(2,1)S(1)}, s16[4,16,2176]{2,1,0:T(8,128)(2,1)S(1)}, u32[]{:S(2)}, u32[]{:S(2)}) collective-permute-start(s16[4,16,2176]{2,1,0:T(8,128)(2,1)S(1)} %get-tuple-element.13), channel_id=1, source_target_pairs={{0,6},{1,15},{2,20},{3,29},{4,34},{5,43},{6,48},{7,57},{8,14},{9,2... | collective-permute-start | bytes 835592 | tf_op jit(solution)/shard_map/ppermute | solution.py:194
  24.3 3.1 %collective-permute-start.2 = (s16[4,16,2176]{2,1,0:T(8,128)(2,1)S(1)}, s16[4,16,2176]{2,1,0:T(8,128)(2,1)S(1)}, u32[]{:S(2)}, u32[]{:S(2)}) collective-permute-start(s16[4,16,2176]{2,1,0:T(8,128)(2,1)S(1)} %get-tuple-element.14), channel_id=1, source_target_pairs={{0,4},{1,13},{2,22},{3,31},{4,32},{5,41},{6,50},{7,59},{8,12},{9,2... | collective-permute-start | bytes 835592 | tf_op jit(solution)/shard_map/ppermute | solution.py:194
  27.5 0.0 collective-permute-done.x_ref
  27.5 6.5 %shard_map.55.rows_ref = f32[8,16,2048]{2,1,0:T(8,128)S(1)} custom-call(s32[320]{0:T(512)S(1)} %or_reduce_fusion.meta, s32[1]{0:T(128)S(6)} %copy.6.count, bf16[8,16,2048]{2,1,0:T(8,128)(2,1)S(1)} %collective-permute-done.x_ref, bf16[320,128,128]{2,1,0:T(8,128)(2,1)} %stored_ref.3), custom_call_target="tpu_custom_call" | custom-call | flops 1000000000 | bytes 12582912 | tf_op jit(solution)/shard_map/pallas_call | solution.py:108
  34.0 12.9 %collective-permute-done.1.refs_0_ = s16[4,16,2176]{2,1,0:T(8,128)(2,1)S(1)} collective-permute-done((s16[4,16,2176]{2,1,0:T(8,128)(2,1)S(1)}, s16[4,16,2176]{2,1,0:T(8,128)(2,1)S(1)}, u32[]{:S(2)}, u32[]{:S(2)}) %collective-permute-start.1) | collective-permute-done | bytes 278560 | tf_op jit(solution)/shard_map/ppermute | solution.py:194
  46.9 0.0 collective-permute-done.2.refs_1_
  46.9 1.8 %shard_map.57 = s16[8,16,2176]{2,1,0:T(8,128)(2,1)S(1)} custom-call(f32[8,16,2048]{2,1,0:T(8,128)S(1)} %shard_map.55.rows_ref, s16[4,16,2176]{2,1,0:T(8,128)(2,1)S(1)} %collective-permute-done.1.refs_0_, s16[4,16,2176]{2,1,0:T(8,128)(2,1)S(1)} %collective-permute-done.2.refs_1_), custom_call_target="tpu_custom_call" | custom-call | tf_op jit(solution)/shard_map/pallas_call | solution.py:170
  48.7 23.0 %all_to_all.11.refs_0_ = s16[8,16,2176]{2,1,0:T(8,128)(2,1)S(1)} all-to-all(s16[8,16,2176]{2,1,0:T(8,128)(2,1)S(1)} %shard_map.57), channel_id=1, replica_groups=mesh['diag'=32,'off'=8] {'off'}, dimensions={0} | all-to-all | bytes 1114112 | tf_op jit(solution)/shard_map/all_to_all | solution.py:198
  71.7 1.0 %shard_map.58 = f32[1,16,2048]{2,1,0:T(8,128)} custom-call(s16[8,16,2176]{2,1,0:T(8,128)(2,1)S(1)} %all_to_all.11.refs_0_), custom_call_target="tpu_custom_call" | custom-call | tf_op jit(solution)/shard_map/pallas_call | solution.py:141
Async XLA Ops:
  14.9 12.6 %collective-permute-start = (bf16[8,16,2048]{2,1,0:T(8,128)(2,1)S(1)}, bf16[8,16,2048]{2,1,0:T(8,128)(2,1)S(1)}, u32[]{:S(2)}, u32[]{:S(2)}) collective-permute-start(bf16[8,16,2048]{2,1,0:T(8,128)(2,1)S(1)} %all_to_all.10.x_ref), channel_id=1, source_target_pairs={{0,0},{9,1},{22,2},{31,3},{36,4},{45,5},{50,6},{59,7},{8,8},{21,9}... | collective-permute-start | bytes 1572872 | tf_op jit(solution)/shard_map/ppermute | solution.py:191
  23.1 23.8 %collective-permute-start.1 = (s16[4,16,2176]{2,1,0:T(8,128)(2,1)S(1)}, s16[4,16,2176]{2,1,0:T(8,128)(2,1)S(1)}, u32[]{:S(2)}, u32[]{:S(2)}) collective-permute-start(s16[4,16,2176]{2,1,0:T(8,128)(2,1)S(1)} %get-tuple-element.13), channel_id=1, source_target_pairs={{0,6},{1,15},{2,20},{3,29},{4,34},{5,43},{6,48},{7,57},{8,14},{9,2... | collective-permute-start | bytes 835592 | tf_op jit(solution)/shard_map/ppermute | solution.py:194
  24.3 22.6 %collective-permute-start.2 = (s16[4,16,2176]{2,1,0:T(8,128)(2,1)S(1)}, s16[4,16,2176]{2,1,0:T(8,128)(2,1)S(1)}, u32[]{:S(2)}, u32[]{:S(2)}) collective-permute-start(s16[4,16,2176]{2,1,0:T(8,128)(2,1)S(1)} %get-tuple-element.14), channel_id=1, source_target_pairs={{0,4},{1,13},{2,22},{3,31},{4,32},{5,41},{6,50},{7,59},{8,12},{9,2... | collective-permute-start | bytes 835592 | tf_op jit(solution)/shard_map/ppermute | solution.py:194

commit v5 on v4

--- a/solution.py
+++ b/solution.py
@@ -33,7 +33,7 @@
         largest = jnp.max(jnp.abs(values), axis=1, keepdims=True)
         power = jnp.floor(jnp.log2(jnp.maximum(largest, 2.0**-112)))
         scaled = jnp.round(values * jnp.exp2(14.0 - power))
-        scaled = jnp.clip(scaled, -32767.0, 32767.0).astype(jnp.int32)
+        scaled = jnp.minimum(scaled, 32767.0).astype(jnp.int32)
         target[part, :, block * TILE : (block + 1) * TILE] = scaled.astype(jnp.int16)
         exponents = jnp.where(lane == block, power.astype(jnp.int32), exponents)
     target[part, :, per_part * TILE :] = exponents.astype(jnp.int16)
@@ -95,7 +95,7 @@
                 quantized(total.at[pl.ds(first * count_sent, count_sent)], sent_ref, part, per_part)
                 return carry
 
-            lax.fori_loop(0, count_sent, part_out, 0)
+            lax.fori_loop(0, count_sent, part_out, 0, unroll=True)
 
 
 def partials(transposed, pieces, meta, count, x, tiles):
@@ -162,7 +162,7 @@
             quantized(total_ref, out_ref, whole, per_part)
             return carry
 
-        lax.fori_loop(0, each, one_part, 0)
+        lax.fori_loop(0, each, one_part, 0, unroll=True)
 
 
 def joined(rows, *arrived):

time: 73.7 us -> 71.4 us (0.969)
  the two profiles are of different devices: /device:TPU:129 before, /device:TPU:33 now
where the time goes in v5:
time: 71.4 us; the launch traced here: 71.5 us
  blocking collectives  33.3 us (47%)
  Pallas kernels  15.5 us (22%)
  waiting for transfers between devices  14.4 us (20%)
  starting transfers between devices  5.9 us (8%)
  local copies, waits for them, and re-layouts  0.88 us (1%)
  other arithmetic  0.79 us (1%)
    all_to_all x1, blocking collectives, per_device(): return summed(lax.all_to_all(joined(rows, *arrived), 'off', 0, 0))[0]  19.3 us
    ppermute x2, waiting for transfers between devices, per_device(): lax.ppermute(piece, AXES, [(at(a, b), at(a + b, home(a + b, b))) for a, b...  14.4 us
    all_to_all x1, blocking collectives, per_device(): x_rows = lax.all_to_all(copies, 'off', 0, 0)  14 us
    pallas_call x2, Pallas kernels, partials(): pl.pallas_call(functools.partial(tiles_kernel, transposed, width // TILE,...  13.2 us
    ppermute x2, starting transfers between devices, per_device(): lax.ppermute(piece, AXES, [(at(a, b), at(a + b, home(a + b, b))) for a, b...  5.21 us
  transfers between devices with their start and end apart: 3, of which 1 were waited for; matrix products, arithmetic and copies ran while one was open for 1% of the time, Pallas kernels for 18%

profile of v5, /device:TPU:33, one launch (start us, length us, event | category | flops | bytes accessed | tf_op | source)
XLA Modules:
  0.0 71.5 jit_solution(16970152954533209640)
XLA Ops:
  0.0 0.9 %broadcast_in_dim.2 = bf16[8,16,2048]{2,1,0:T(8,128)(2,1)S(1)} broadcast(bf16[16,2048]{1,0:T(8,128)(2,1)} %param.5), dimensions={1,2} | broadcast | bytes 589824 | tf_op jit(solution)/shard_map/broadcast_in_dim | solution.py:187
  0.9 14.0 %all_to_all.10.x_ref = bf16[8,16,2048]{2,1,0:T(8,128)(2,1)S(1)} all-to-all(bf16[8,16,2048]{2,1,0:T(8,128)(2,1)S(1)} %broadcast_in_dim.2), channel_id=1, replica_groups=mesh['diag'=32,'off'=8] {'off'}, dimensions={0} | all-to-all | bytes 1048576 | tf_op jit(solution)/shard_map/all_to_all | solution.py:188
  14.9 0.7 collective-permute-start
  16.2 0.8 %or_reduce_fusion.meta = s32[320]{0:T(512)S(1)} fusion(s32[320,2]{0,1:T(2,128)} %param.8, s32[320,2]{0,1:T(2,128)} %param.7), kind=kLoop, calls=%fused_computation | loop fusion | flops 1920 | bytes 6400 | tf_op jit(solution)/shard_map/or | solution.py:190
  17.0 6.0 %shard_map.56 = (s16[4,16,2176]{2,1,0:T(8,128)(2,1)S(1)}, s16[4,16,2176]{2,1,0:T(8,128)(2,1)S(1)}) custom-call(s32[320]{0:T(512)S(1)} %or_reduce_fusion.meta, s32[1]{0:T(128)S(6)} %copy.6.count, bf16[8,16,2048]{2,1,0:T(8,128)(2,1)S(1)} %all_to_all.10.x_ref, bf16[320,128,128]{2,1,0:T(8,128)(2,1)} %stored_ref.3), custom_call_target="tpu_custom_call" | custom-call | flops 1000000000 | bytes 12582912 | tf_op jit(solution)/shard_map/pallas_call | solution.py:108
  23.0 3.4 %collective-permute-start.1 = (s16[4,16,2176]{2,1,0:T(8,128)(2,1)S(1)}, s16[4,16,2176]{2,1,0:T(8,128)(2,1)S(1)}, u32[]{:S(2)}, u32[]{:S(2)}) collective-permute-start(s16[4,16,2176]{2,1,0:T(8,128)(2,1)S(1)} %get-tuple-element.13), channel_id=1, source_target_pairs={{0,6},{1,15},{2,20},{3,29},{4,34},{5,43},{6,48},{7,57},{8,14},{9,2... | collective-permute-start | bytes 835592 | tf_op jit(solution)/shard_map/ppermute | solution.py:194
  26.4 1.8 %collective-permute-start.2 = (s16[4,16,2176]{2,1,0:T(8,128)(2,1)S(1)}, s16[4,16,2176]{2,1,0:T(8,128)(2,1)S(1)}, u32[]{:S(2)}, u32[]{:S(2)}) collective-permute-start(s16[4,16,2176]{2,1,0:T(8,128)(2,1)S(1)} %get-tuple-element.14), channel_id=1, source_target_pairs={{0,4},{1,13},{2,22},{3,31},{4,32},{5,41},{6,50},{7,59},{8,12},{9,2... | collective-permute-start | bytes 835592 | tf_op jit(solution)/shard_map/ppermute | solution.py:194
  28.2 0.0 collective-permute-done.x_ref
  28.2 7.2 %shard_map.55.rows_ref = f32[8,16,2048]{2,1,0:T(8,128)S(1)} custom-call(s32[320]{0:T(512)S(1)} %or_reduce_fusion.meta, s32[1]{0:T(128)S(6)} %copy.6.count, bf16[8,16,2048]{2,1,0:T(8,128)(2,1)S(1)} %collective-permute-done.x_ref, bf16[320,128,128]{2,1,0:T(8,128)(2,1)} %stored_ref.3), custom_call_target="tpu_custom_call" | custom-call | flops 1000000000 | bytes 12582912 | tf_op jit(solution)/shard_map/pallas_call | solution.py:108
  35.5 14.4 %collective-permute-done.1.refs_0_ = s16[4,16,2176]{2,1,0:T(8,128)(2,1)S(1)} collective-permute-done((s16[4,16,2176]{2,1,0:T(8,128)(2,1)S(1)}, s16[4,16,2176]{2,1,0:T(8,128)(2,1)S(1)}, u32[]{:S(2)}, u32[]{:S(2)}) %collective-permute-start.1) | collective-permute-done | bytes 278560 | tf_op jit(solution)/shard_map/ppermute | solution.py:194
  49.9 0.0 collective-permute-done.2.refs_1_
  49.9 1.2 %shard_map.57 = s16[8,16,2176]{2,1,0:T(8,128)(2,1)S(1)} custom-call(f32[8,16,2048]{2,1,0:T(8,128)S(1)} %shard_map.55.rows_ref, s16[4,16,2176]{2,1,0:T(8,128)(2,1)S(1)} %collective-permute-done.1.refs_0_, s16[4,16,2176]{2,1,0:T(8,128)(2,1)S(1)} %collective-permute-done.2.refs_1_), custom_call_target="tpu_custom_call" | custom-call | tf_op jit(solution)/shard_map/pallas_call | solution.py:170
  51.1 19.3 %all_to_all.11.refs_0_ = s16[8,16,2176]{2,1,0:T(8,128)(2,1)S(1)} all-to-all(s16[8,16,2176]{2,1,0:T(8,128)(2,1)S(1)} %shard_map.57), channel_id=1, replica_groups=mesh['diag'=32,'off'=8] {'off'}, dimensions={0} | all-to-all | bytes 1114112 | tf_op jit(solution)/shard_map/all_to_all | solution.py:198
  70.4 1.0 %shard_map.58 = f32[1,16,2048]{2,1,0:T(8,128)} custom-call(s16[8,16,2176]{2,1,0:T(8,128)(2,1)S(1)} %all_to_all.11.refs_0_), custom_call_target="tpu_custom_call" | custom-call | tf_op jit(solution)/shard_map/pallas_call | solution.py:141
Async XLA Ops:
  14.9 13.3 %collective-permute-start = (bf16[8,16,2048]{2,1,0:T(8,128)(2,1)S(1)}, bf16[8,16,2048]{2,1,0:T(8,128)(2,1)S(1)}, u32[]{:S(2)}, u32[]{:S(2)}) collective-permute-start(bf16[8,16,2048]{2,1,0:T(8,128)(2,1)S(1)} %all_to_all.10.x_ref), channel_id=1, source_target_pairs={{0,0},{9,1},{22,2},{31,3},{36,4},{45,5},{50,6},{59,7},{8,8},{21,9}... | collective-permute-start | bytes 1572872 | tf_op jit(solution)/shard_map/ppermute | solution.py:191
  23.0 26.8 %collective-permute-start.1 = (s16[4,16,2176]{2,1,0:T(8,128)(2,1)S(1)}, s16[4,16,2176]{2,1,0:T(8,128)(2,1)S(1)}, u32[]{:S(2)}, u32[]{:S(2)}) collective-permute-start(s16[4,16,2176]{2,1,0:T(8,128)(2,1)S(1)} %get-tuple-element.13), channel_id=1, source_target_pairs={{0,6},{1,15},{2,20},{3,29},{4,34},{5,43},{6,48},{7,57},{8,14},{9,2... | collective-permute-start | bytes 835592 | tf_op jit(solution)/shard_map/ppermute | solution.py:194
  26.4 23.4 %collective-permute-start.2 = (s16[4,16,2176]{2,1,0:T(8,128)(2,1)S(1)}, s16[4,16,2176]{2,1,0:T(8,128)(2,1)S(1)}, u32[]{:S(2)}, u32[]{:S(2)}) collective-permute-start(s16[4,16,2176]{2,1,0:T(8,128)(2,1)S(1)} %get-tuple-element.14), channel_id=1, source_target_pairs={{0,4},{1,13},{2,22},{3,31},{4,32},{5,41},{6,50},{7,59},{8,12},{9,2... | collective-permute-start | bytes 835592 | tf_op jit(solution)/shard_map/ppermute | solution.py:194
